TPU v7x, 256 devices: a whole 4x4x8 slice. The times are simulated.
256 devices in a mesh: narrow: 4 (over z_lo, core), wide: 64 (over z_hi, x, y).
Axes of the slice: x: 4, y: 4, z: 8 (z_hi: 4, z_lo: 2; z = z_hi * 2 + z_lo), core: 2. Of those that a mesh axis runs over, the one named last changes fastest.
Arguments:
- tokens: bfloat16 [512, 16384], P('narrow', 'wide'), may hold values from -6 to 6
- w_query: bfloat16 [16384, 8192], P('wide', 'narrow'), may hold values from -0.046875 to 0.046875
- w_keyval: bfloat16 [16384, 1024], P('wide', 'narrow'), may hold values from -0.046875 to 0.046875
- w_output: bfloat16 [8192, 16384], P('narrow', 'wide'), may hold values from -0.0625 to 0.0625
- grad_out: bfloat16 [512, 16384], P('narrow', 'wide'), may hold values from -6 to 6
Outputs:
- output: bfloat16 [512, 16384], P('narrow', 'wide')
- grad_tokens: bfloat16 [512, 16384], P('narrow', 'wide')
- grad_wq: bfloat16 [16384, 8192], P('wide', 'narrow')
- grad_wkv: bfloat16 [16384, 1024], P('wide', 'narrow')
- grad_wo: bfloat16 [8192, 16384], P('narrow', 'wide')
All inputs are finite; a program needn't handle non-finite values.
Results may differ from a plain program's by a relative error of at most 0.015.
Values may be sent and summed in bfloat16 or wider, within the bound.
A program may use at most 64 MiB of HBM per device.

v0:
```python
import jax
import jax.numpy as jnp
from jax import lax
from jax.sharding import PartitionSpec as P

HD = 128


def contract_rows(left, right):
    return lax.dot_general(
        left, right, (((0,), (0,)), ((), ())), preferred_element_type=jnp.float32
    )


def contract_cols(left, right):
    return lax.dot_general(
        left, right, (((1,), (1,)), ((), ())), preferred_element_type=jnp.float32
    )


def wide_sum(term_fn, all_rows):
    return lax.psum_scatter(
        term_fn(jnp.int32(0), lax.axis_size("wide") * (all_rows // lax.axis_size("wide"))),
        "wide",
        scatter_dimension=0,
        tiled=True,
    )


def shards(tokens, w_query, w_keyval, w_output, grad_out):
    wide_index = lax.axis_index("wide")
    token_panel = lax.all_gather(tokens, "narrow", axis=0, tiled=True)
    all_rows = token_panel.shape[0]
    query_cols = w_query.shape[1]
    pair_cols = w_keyval.shape[1]
    joined = jnp.concatenate([w_query, w_keyval], axis=1)

    def project_all(first_row, row_count):
        return jnp.dot(token_panel, joined, preferred_element_type=jnp.float32)

    projected = wide_sum(project_all, all_rows)
    queries = projected[:, :query_cols].astype(jnp.bfloat16)
    kv_own = projected[:, query_cols:].astype(jnp.bfloat16)
    kv_panel = lax.all_gather(kv_own, "wide", axis=0, tiled=True)
    rows_here = queries.shape[0]
    heads_here = query_cols // HD
    groups_here = pair_cols // (2 * HD)
    group_size = heads_here // groups_here
    score_scale = HD ** (-0.5)
    query_pos = wide_index * rows_here + lax.iota(jnp.int32, rows_here)
    key_pos = lax.iota(jnp.int32, all_rows)
    allowed = key_pos[None, :] <= query_pos[:, None]
    query_heads = queries.reshape(rows_here, groups_here, group_size, HD)
    pair_heads = kv_panel.reshape(all_rows, groups_here, 2, HD)
    key_heads = pair_heads[:, :, 0]
    value_heads = pair_heads[:, :, 1]
    scores = (
        jnp.einsum("rghd,sgd->ghrs", query_heads, key_heads, preferred_element_type=jnp.float32)
        * score_scale
    )
    weights = jnp.where(allowed, jnp.exp(scores), 0.0)
    weights = weights / jnp.sum(weights, axis=3, keepdims=True)
    prob_bf = weights.astype(jnp.bfloat16)
    attended = jnp.einsum(
        "ghrs,sgd->rghd", prob_bf, value_heads, preferred_element_type=jnp.float32
    )
    attended = attended.reshape(rows_here, query_cols).astype(jnp.bfloat16)
    att_panel = lax.all_gather(attended, "wide", axis=0, tiled=True)
    row_block = att_panel
    output = lax.psum_scatter(
        jnp.dot(row_block, w_output, preferred_element_type=jnp.float32).astype(jnp.bfloat16),
        "narrow",
        scatter_dimension=0,
        tiled=True,
    )
    grad_panel = lax.all_gather(grad_out, "narrow", axis=0, tiled=True)
    grad_wo = contract_rows(att_panel, grad_panel).astype(jnp.bfloat16)

    def back_out(first_row, row_count):
        return contract_cols(grad_panel, w_output)

    grad_att = wide_sum(back_out, all_rows).astype(jnp.bfloat16)
    grad_heads = grad_att.reshape(rows_here, groups_here, group_size, HD)
    prob_grad = jnp.einsum(
        "rghd,sgd->ghrs", grad_heads, value_heads, preferred_element_type=jnp.float32
    )
    grad_values = jnp.einsum(
        "ghrs,rghd->sgd", prob_bf, grad_heads, preferred_element_type=jnp.float32
    )
    score_grad = weights * (prob_grad - jnp.sum(weights * prob_grad, axis=3, keepdims=True))
    score_half = score_grad.astype(jnp.bfloat16)
    grad_q = (
        jnp.einsum("ghrs,sgd->rghd", score_half, key_heads, preferred_element_type=jnp.float32)
        * score_scale
    )
    grad_q = grad_q.reshape(rows_here, query_cols).astype(jnp.bfloat16)
    grad_keys = (
        jnp.einsum("ghrs,rghd->sgd", score_half, query_heads, preferred_element_type=jnp.float32)
        * score_scale
    )
    kv_grad = jnp.stack([grad_keys, grad_values], axis=2).reshape(all_rows, pair_cols)
    kv_share = lax.psum_scatter(kv_grad, "wide", scatter_dimension=0, tiled=True).astype(
        jnp.bfloat16
    )
    grad_mixed = jnp.concatenate([grad_q, kv_share], axis=1)
    grad_rows = lax.all_gather(grad_mixed, "wide", axis=0, tiled=True)
    grad_joined = contract_rows(token_panel, grad_rows)
    grad_wq = grad_joined[:, :query_cols].astype(jnp.bfloat16)
    grad_wkv = grad_joined[:, query_cols:].astype(jnp.bfloat16)
    row_block = grad_rows
    grad_tokens = lax.psum_scatter(
        contract_cols(row_block, joined).astype(jnp.bfloat16),
        "narrow",
        scatter_dimension=0,
        tiled=True,
    )
    return (output, grad_tokens, grad_wq, grad_wkv, grad_wo)


def solution(mesh):
    return jax.shard_map(
        shards,
        mesh=mesh,
        in_specs=(
            P("narrow", "wide"),
            P("wide", "narrow"),
            P("wide", "narrow"),
            P("narrow", "wide"),
            P("narrow", "wide"),
        ),
        out_specs=(
            P("narrow", "wide"),
            P("narrow", "wide"),
            P("wide", "narrow"),
            P("wide", "narrow"),
            P("narrow", "wide"),
        ),
        check_vma=False,
    )
```

profile of v0, /device:TPU:1, one launch (start us, length us, event | category | flops | bytes accessed | tf_op | source)
XLA Modules:
  0.0 1442.6 jit_solution(16058922875127216114)
XLA Ops:
  7.2 9.2 all_gather.18
  16.4 2.8 fusion.13
  19.3 0.0 reduce-scatter.16.cloned.1.call-start
  19.3 0.8 copy-done.5
  20.1 6.0 all_gather.15
  26.1 0.1 constant_dynamic-update-slice_fusion.1
  26.2 3.0 convolution_bitcast_fusion
  29.2 6.1 copy.37
  35.4 0.0 reduce-scatter.12.cloned.1.call-start
  35.4 0.1 iota_compare_fusion
  35.5 326.2 %reduce-scatter.10.cloned.1.call-done = f32[8,2048]{1,0:T(8,128)} async-done(((f32[512,2048]{1,0:T(8,128)}), f32[8,2048]{1,0:T(8,128)}) %reduce-scatter.10.cloned.1.call-update) | async-done | bytes 65552 | tf_op jit(solution)/shard_map/reduce_scatter | solution.py:22
  361.7 0.8 convert_bitcast_fusion.1
  362.6 299.1 %reduce-scatter.16.cloned.1.call-done = f32[8,2304]{1,0:T(8,128)} async-done(((f32[512,2304]{1,0:T(8,128)}), f32[8,2304]{1,0:T(8,128)}) %reduce-scatter.16.cloned.1.call-update) | async-done | bytes 73744
  661.7 0.7 slice.28
  662.4 0.1 copy.55
  662.5 0.1 copy.39
  662.6 162.6 %all_gather.16 = bf16[512,256]{1,0:T(8,128)(2,1)S(1)} all-gather(bf16[8,256]{1,0:T(8,128)(2,1)S(1)} %copy.39), channel_id=1, replica_groups=mesh['narrow'=4,'wide'=64] {'wide'}, dimensions={0}, use_global_device_ids=true | all-gather | bytes 266240 | tf_op jit(solution)/shard_map/all_gather | solution.py:44
  825.1 0.1 copy.27
  825.3 0.8 slice.31
  826.1 0.3 copy.54
  826.4 0.2 copy.36
  826.6 0.3 fusion.12
  826.9 0.3 multiply_reduce_fusion
  827.1 0.1 fusion.9
  827.3 0.2 fusion.5
  827.5 0.2 convolution_bitcast_fusion.1
  827.8 1.0 copy.33
  828.8 0.0 all-gather.3.cloned.1.call-start
  828.8 0.2 fusion.7
  829.0 0.6 copy.53
  829.7 0.0 all-gather.5.cloned.1.call-start
  829.7 0.2 fusion.8
  829.9 352.2 %reduce-scatter.12.cloned.1.call-done = f32[8,256]{1,0:T(8,128)} async-done(((f32[512,256]{1,0:T(8,128)}), f32[8,256]{1,0:T(8,128)}) %reduce-scatter.12.cloned.1.call-update) | async-done | bytes 8208 | tf_op jit(solution)/shard_map/reduce_scatter | solution.py:102
  1182.1 0.7 convert_element_type.61
  1182.8 0.6 pad_maximum_fusion.1
  1183.5 0.0 reduce-scatter.8.cloned.1.call-start
  1183.5 125.1 %all-gather.3.cloned.1.call-done = bf16[512,2048]{1,0:T(8,128)(2,1)} async-done(((bf16[8,2048]{1,0:T(8,128)(2,1)}), bf16[512,2048]{1,0:T(8,128)(2,1)}) %all-gather.3.cloned.1.call-update) | async-done | bytes 2097168 | tf_op jit(solution)/shard_map/all_gather | solution.py:68
  1308.6 3.0 convolution_convert_fusion.3
  1311.7 0.0 reduce-scatter.14.cloned.1.call-start
  1311.7 77.8 %all-gather.5.cloned.1.call-done = bf16[512,2304]{1,0:T(8,128)(2,1)} async-done(((bf16[8,2304]{1,0:T(8,128)(2,1)}), bf16[512,2304]{1,0:T(8,128)(2,1)}) %all-gather.5.cloned.1.call-update) | async-done | bytes 2359312 | tf_op jit(solution)/shard_map/all_gather | solution.py:106
  1389.5 3.2 convolution_convert_fusion.2
  1392.7 3.5 convolution_convert_fusion.1
  1396.2 0.8 fusion
  1397.0 0.1 slice.32
  1397.1 1.4 copy.34
  1398.5 0.8 copy.35
  1399.3 12.9 reduce-scatter.8.cloned.1.call-done
  1412.2 23.6 %reduce-scatter.14.cloned.1.call-done = bf16[128,256]{1,0:T(8,128)(2,1)} async-done(((bf16[512,256]{1,0:T(8,128)(2,1)}), bf16[128,256]{1,0:T(8,128)(2,1)}) %reduce-scatter.14.cloned.1.call-update) | async-done | bytes 65552 | tf_op jit(solution)/shard_map/reduce_scatter | solution.py:111
  (26 shorter events, 0.3 us)
Async XLA Ops:
  7.2 9.3 copy-start
  7.2 354.6 %reduce-scatter.10.cloned.1.call-start = ((), (), s32[]{:S(2)}) async-start(), calls=%async_computation.7 | async-start | bytes 4259840 | tf_op jit(solution)/shard_map/reduce_scatter | solution.py:22
  16.4 2.8 copy-start.2
  19.3 0.8 copy-start.5
  19.3 6.8 copy-start.1
  19.3 642.4 %reduce-scatter.16.cloned.1.call-start = ((), (), s32[]{:S(2)}) async-start(), calls=%async_computation.11 | async-start | bytes 4792320
  20.1 6.1 copy-start.4
  35.4 1146.8 %reduce-scatter.12.cloned.1.call-start = ((), (), s32[]{:S(2)}) async-start(), calls=%async_computation.8 | async-start | bytes 532480 | tf_op jit(solution)/shard_map/reduce_scatter | solution.py:102
  828.8 479.9 %all-gather.3.cloned.1.call-start = ((), (), s32[]{:S(2)}) async-start(), calls=%async_computation.5 | async-start | bytes 2129920 | tf_op jit(solution)/shard_map/all_gather | solution.py:68
  829.7 559.8 %all-gather.5.cloned.1.call-start = ((), (), s32[]{:S(2)}) async-start(), calls=%async_computation.9 | async-start | bytes 2396160 | tf_op jit(solution)/shard_map/all_gather | solution.py:106
  1183.5 228.8 %reduce-scatter.8.cloned.1.call-start = ((), (), s32[]{:S(2)}) async-start(), calls=%async_computation.6 | async-start | bytes 327680 | tf_op jit(solution)/shard_map/reduce_scatter | solution.py:70
  1311.7 81.0 %copy-start.3 = (bf16[512,256]{1,0:T(8,128)(2,1)S(1)}, bf16[512,256]{1,0:T(8,128)(2,1)}, u32[]{:S(2)}) copy-start(bf16[512,256]{1,0:T(8,128)(2,1)} %copy-done.2) | copy-start | bytes 786436
  1311.7 124.1 %reduce-scatter.14.cloned.1.call-start = ((), (), s32[]{:S(2)}) async-start(), calls=%async_computation.10 | async-start | bytes 327680 | tf_op jit(solution)/shard_map/reduce_scatter | solution.py:111
  1392.7 3.5 copy-start.6
Sparse Core Ops, SparseCore 0:
  19.4 342.2 reduce-scatter.9
  367.4 294.2 reduce-scatter.15
  828.9 353.1 reduce-scatter.11
  1185.8 122.7 all-gather.2
  1312.2 77.2 all-gather.4
  1392.4 19.7 reduce-scatter.7
  1415.5 20.2 reduce-scatter.13
where the time goes:
time: 1440 us
  waiting for transfers between devices  1220 us (85%)
  blocking collectives  178 us (12%)
  matrix products  17.6 us (1%)
    reduce_scatter x1, waiting for transfers between devices, shards(): lax.psum_scatter(kv_grad, 'wide', scatter_dimension=0, tiled=True)  352 us
    reduce_scatter x1, waiting for transfers between devices, wide_sum(): lax.psum_scatter(term_fn(jnp.int32(0), lax.axis_size('wide') * (all_rows...  326 us
    unnamed x8, waiting for transfers between devices  299 us
    all_gather x1, blocking collectives, shards(): kv_panel = lax.all_gather(kv_own, 'wide', axis=0, tiled=True)  163 us
    all_gather x1, waiting for transfers between devices, shards(): att_panel = lax.all_gather(attended, 'wide', axis=0, tiled=True)  125 us
    all_gather x1, waiting for transfers between devices, shards(): grad_rows = lax.all_gather(grad_mixed, 'wide', axis=0, tiled=True)  77.8 us
  transfers between devices with their start and end apart: 7, of which 7 were waited for; matrix products, arithmetic and copies ran while one was open for 2% of the time, Pallas kernels for 0%

commit v1 on v0

v1 whole, which is shorter than its diff:
```python
import functools

import jax
import jax.numpy as jnp
from jax import lax
from jax.experimental import pallas as pl
from jax.experimental.pallas import tpu as pltpu
from jax.sharding import PartitionSpec as P

HD = 128
F32 = jnp.float32
BF16 = jnp.bfloat16
MESH = pl.DeviceIdType.MESH
SEMS = 160


def mm(left, right, dims):
    return lax.dot_general(left, right, (dims, ((), ())), preferred_element_type=F32)


NN = ((1,), (0,))
NT = ((1,), (1,))
TN = ((0,), (0,))


def kernel(
    K, N, tok, wq_h, wkv_h, wo_h, gout,
    out_h, gtok_h, gwq_h, gwkv_h, gwo_h,
    wq, wkv, wo, tpan, gpan, pq, pg, pkv, pkg,
    q1, qs1, q2, qs2, q3, qf,
    g1, gs1, g2, gs2, g3, gf,
    k1, ks1, k2, ks2, k3,
    m1, ms1, m2, ms2, m3,
    kvp, kgp, ap, dp, o_part, o_recv, t_part, t_recv,
    o_out, t_out, gwq_o, gwkv_o, gwo_o,
    send_sems, recv_sems, local_sems,
):
    Z = K
    R, U = pq.shape[3], pq.shape[4]
    rows = K * K * R
    C = 2 * Z
    me = lax.axis_index("wide")
    nar = lax.axis_index("narrow")
    z, x, y = me // (K * K), (me // K) % K, me % K
    part_rows = rows // N

    def peer(axis, d):
        if axis == "n":
            i = (nar + d) % N
            return {"narrow": i}, i
        if axis == "z":
            i = (z + d) % K
            return {"wide": i * K * K + x * K + y}, i
        if axis == "x":
            i = (x + d) % K
            return {"wide": z * K * K + i * K + y}, i
        i = (y + d) % K
        return {"wide": z * K * K + x * K + i}, i

    count = [0]
    sent = []

    def send(axis, src, dst):
        copies = []
        for d in range(1, N if axis == "n" else K):
            device, place = peer(axis, d)
            i = count[0]
            count[0] += 1
            c = pltpu.make_async_remote_copy(
                src_ref=src(place), dst_ref=dst(d),
                send_sem=send_sems.at[i], recv_sem=recv_sems.at[i],
                device_id=device, device_id_type=MESH,
            )
            c.start()
            copies.append(c)
        sent.extend(copies)
        return copies

    def arrived(copies):
        for c in copies:
            c.wait_recv()

    loads = []
    for i, (s, d) in enumerate(
        [(tok, tpan.at[nar]), (gout, gpan.at[nar]), (wkv_h, wkv), (wq_h, wq), (wo_h, wo)]
    ):
        c = pltpu.make_async_copy(s, d, local_sems.at[i])
        c.start()
        loads.append(c)

    barrier = pltpu.get_barrier_semaphore()
    peers = [("n", d) for d in range(1, N)] + [(a, d) for a in "zxy" for d in range(1, K)]
    for a, d in peers:
        pl.semaphore_signal(barrier, inc=1, device_id=peer(a, d)[0], device_id_type=MESH)
    pl.semaphore_wait(barrier, len(peers))

    tok_c = send("n", lambda p: tok, lambda d: tpan.at[nar])
    gout_c = send("n", lambda p: gout, lambda d: gpan.at[nar])

    first = ("x", "y")
    second = ("y", "x")

    def rs_send1(p, recv, h, per):
        u = slice(h * per, (h + 1) * per)
        if h == 0:
            return send("x", lambda i: p.at[u, i], lambda d: recv.at[h, d - 1])
        return send("y", lambda i: p.at[u, :, i], lambda d: recv.at[h, d - 1])

    def rs_sum1(p, recv, s, h, per):
        def body(u, _):
            own = p[h * per + u, x] if h == 0 else p[h * per + u, :, y]
            total = own.astype(F32)
            for d in range(K - 1):
                total += recv[h, d, u].astype(F32)
            s[h, u] = total.astype(BF16)
            return 0

        lax.fori_loop(0, per, body, 0)

    def rs_send2(s, recv, h):
        return send(second[h], lambda i: s.at[h, :, i], lambda d: recv.at[h, d - 1])

    def rs_sum2(s, recv, t, h):
        own = s[h, :, y] if h == 0 else s[h, :, x]
        total = own.astype(F32)
        for d in range(K - 1):
            total += recv[h, d].astype(F32)
        t[h] = total.astype(BF16)

    def ag_send2(p, h, per):
        here = p.at[h * per:(h + 1) * per, x, y]
        return send(second[h], lambda i: here, lambda d: here)

    def ag_send3(p, h, per):
        u = slice(h * per, (h + 1) * per)
        here = p.at[u, x] if h == 0 else p.at[u, :, y]
        return send(first[h], lambda i: here, lambda d: here)

    both = (0, 1)

    arrived(tok_c)
    for i in (0, 2, 3):
        loads[i].wait()
    tokens = tpan[...].reshape(rows, -1)
    kv = mm(tokens, wkv[...], NN).astype(BF16)
    for h in both:
        pkv[h] = kv[:, h * HD:(h + 1) * HD].reshape(K, K, R, HD)
    k1_c = [rs_send1(pkv, k1, h, 1) for h in both]
    q1_c = []
    for h in both:
        for c in range(h * Z, (h + 1) * Z):
            pq[c] = mm(tokens, wq[:, c * U:(c + 1) * U], NN).astype(BF16).reshape(K, K, R, U)
        q1_c.append(rs_send1(pq, q1, h, Z))
    arrived(gout_c)
    for i in (1, 4):
        loads[i].wait()
    grads = gpan[...].reshape(rows, -1)
    g1_c = []
    for h in both:
        for c in range(h * Z, (h + 1) * Z):
            pg[c] = mm(grads, wo[c * U:(c + 1) * U, :], NT).astype(BF16).reshape(K, K, R, U)
        g1_c.append(rs_send1(pg, g1, h, Z))

    k2_c = []
    for h in both:
        arrived(k1_c[h])
        rs_sum1(pkv, k1, ks1, h, 1)
        k2_c.append(rs_send2(ks1, k2, h))
    q2_c = []
    for h in both:
        arrived(q1_c[h])
        rs_sum1(pq, q1, qs1, h, Z)
        q2_c.append(rs_send2(qs1, q2, h))

    def share_z(s, recv, h):
        return send("z", lambda i: s.at[h], lambda d: recv.at[h, d - 1])

    def finish_shared(s, recv, p, h):
        total = s[h].astype(F32)
        for d in range(K - 1):
            total += recv[h, d].astype(F32)
        p[h, x, y] = total.astype(BF16)[0]

    def rs_send3(s, recv, h):
        return send("z", lambda i: s.at[h, i], lambda d: recv.at[h, d - 1])

    def rs_finish(s, recv, f, h):
        total = s[h, z].astype(F32)
        for d in range(K - 1):
            total += recv[h, d].astype(F32)
        f[h] = total.astype(BF16)

    k3_c = []
    for h in both:
        arrived(k2_c[h])
        rs_sum2(ks1, k2, ks2, h)
        k3_c.append(share_z(ks2, k3, h))
    q3_c = []
    for h in both:
        arrived(q2_c[h])
        rs_sum2(qs1, q2, qs2, h)
        q3_c.append(rs_send3(qs2, q3, h))
    ka_c = []
    for h in both:
        arrived(k3_c[h])
        finish_shared(ks2, k3, kvp, h)
        ka_c.append(ag_send2(kvp, h, 1))
    kb_c = []
    for h in both:
        arrived(ka_c[h])
        kb_c.append(ag_send3(kvp, h, 1))
    for h in both:
        arrived(q3_c[h])
        rs_finish(qs2, q3, qf, h)
    for h in both:
        arrived(kb_c[h])

    def heads(f):
        return jnp.concatenate(
            [f[h, :, k * HD:(k + 1) * HD] for h in both for k in range(U // HD)], axis=0
        )

    def unheads(p, v):
        per = U // HD
        for h in both:
            p[h * Z + z, x, y] = jnp.concatenate(
                [v[(h * per + k) * R:(h * per + k + 1) * R] for k in range(per)], axis=1
            )

    scale = HD ** (-0.5)
    queries = heads(qf)
    keys = kvp[0].reshape(rows, HD)
    values = kvp[1].reshape(rows, HD)
    scores = mm(queries, keys, NT) * scale
    place = lax.broadcasted_iota(jnp.int32, scores.shape, 0) % R + (x * K + y) * R
    allowed = lax.broadcasted_iota(jnp.int32, scores.shape, 1) <= place
    weights = jnp.where(allowed, jnp.exp(scores), 0.0)
    weights = weights / jnp.sum(weights, axis=1, keepdims=True)
    probs = weights.astype(BF16)
    unheads(ap, mm(probs, values, NN).astype(BF16))

    def ag_send1(p, h):
        here = p.at[h * Z + z, x, y]
        return send("z", lambda i: here, lambda d: here)

    a1_c = [ag_send1(ap, h) for h in both]

    g2_c = []
    for h in both:
        arrived(g1_c[h])
        rs_sum1(pg, g1, gs1, h, Z)
        g2_c.append(rs_send2(gs1, g2, h))
    g3_c = []
    for h in both:
        arrived(g2_c[h])
        rs_sum2(gs1, g2, gs2, h)
        g3_c.append(rs_send3(gs2, g3, h))
    a2_c = []
    for h in both:
        arrived(a1_c[h])
        a2_c.append(ag_send2(ap, h, Z))
    for h in both:
        arrived(g3_c[h])
        rs_finish(gs2, g3, gf, h)

    cotangent = heads(gf)
    prob_grad = mm(cotangent, values, NT)
    score_grad = weights * (prob_grad - jnp.sum(weights * prob_grad, axis=1, keepdims=True))
    score_half = score_grad.astype(BF16)
    grad_keys = mm(score_half, queries, TN) * scale
    grad_values = mm(probs, cotangent, TN)
    pkg[0] = grad_keys.astype(BF16).reshape(K, K, R, HD)
    pkg[1] = grad_values.astype(BF16).reshape(K, K, R, HD)
    m1_c = [rs_send1(pkg, m1, h, 1) for h in both]
    unheads(dp, (mm(score_half, keys, NN) * scale).astype(BF16))
    d1_c = [ag_send1(dp, h) for h in both]

    m2_c = []
    for h in both:
        arrived(m1_c[h])
        rs_sum1(pkg, m1, ms1, h, 1)
        m2_c.append(rs_send2(ms1, m2, h))
    d2_c = []
    for h in both:
        arrived(d1_c[h])
        d2_c.append(ag_send2(dp, h, Z))
    m3_c = []
    for h in both:
        arrived(m2_c[h])
        rs_sum2(ms1, m2, ms2, h)
        m3_c.append(share_z(ms2, m3, h))
    a3_c = []
    for h in both:
        arrived(a2_c[h])
        a3_c.append(ag_send3(ap, h, Z))
    ma_c = []
    for h in both:
        arrived(m3_c[h])
        finish_shared(ms2, m3, kgp, h)
        ma_c.append(ag_send2(kgp, h, 1))
    d3_c = []
    for h in both:
        arrived(d2_c[h])
        d3_c.append(ag_send3(dp, h, Z))
    mb_c = []
    for h in both:
        arrived(ma_c[h])
        mb_c.append(ag_send3(kgp, h, 1))

    def unit(p, c):
        return p[c].reshape(rows, U)

    def sum_narrow(part, recv, o):
        total = part[nar].astype(F32)
        for d in range(N - 1):
            total += recv[d].astype(F32)
        o[...] = total.astype(BF16)

    stores = []

    def store(s, d):
        c = pltpu.make_async_copy(s, d, local_sems.at[5 + len(stores)])
        c.start()
        stores.append(c)

    total = None
    for h in both:
        arrived(a3_c[h])
        for c in range(h * Z, (h + 1) * Z):
            term = mm(unit(ap, c), wo[c * U:(c + 1) * U, :], NN)
            total = term if total is None else total + term
    o_part[...] = total.astype(BF16).reshape(N, part_rows, -1)
    o_c = send("n", lambda i: o_part.at[i], lambda d: o_recv.at[d - 1])
    for c in range(C):
        gwo_o[c * U:(c + 1) * U, :] = mm(unit(ap, c), grads, TN).astype(BF16)
    store(gwo_o, gwo_h)
    arrived(o_c)
    sum_narrow(o_part, o_recv, o_out)
    store(o_out, out_h)

    total = None
    for h in both:
        arrived(d3_c[h])
        for c in range(h * Z, (h + 1) * Z):
            term = mm(unit(dp, c), wq[:, c * U:(c + 1) * U], NT)
            total = term if total is None else total + term
    for h in both:
        arrived(mb_c[h])
    kv_grad = jnp.concatenate([kgp[h].reshape(rows, HD) for h in both], axis=1)
    total = total + mm(kv_grad, wkv[...], NT)
    t_part[...] = total.astype(BF16).reshape(N, part_rows, -1)
    t_c = send("n", lambda i: t_part.at[i], lambda d: t_recv.at[d - 1])
    tokens_t = tpan[...].reshape(rows, -1)
    for c in range(C):
        gwq_o[:, c * U:(c + 1) * U] = mm(tokens_t, unit(dp, c), TN).astype(BF16)
    store(gwq_o, gwq_h)
    gwkv_o[...] = mm(tokens_t, kv_grad, TN).astype(BF16)
    store(gwkv_o, gwkv_h)
    arrived(t_c)
    sum_narrow(t_part, t_recv, t_out)
    store(t_out, gtok_h)
    for c in stores:
        c.wait()
    for c in sent:
        c.wait_send()


def shards(K, N, tokens, w_query, w_keyval, w_output, grad_out):
    part_rows, feat = tokens.shape
    rows = part_rows * N
    R = rows // (K * K)
    qc = w_query.shape[1]
    Z = K
    C = 2 * Z
    U = qc // C
    assert w_keyval.shape[1] == 2 * HD and U % HD == 0

    def v(*shape):
        return pltpu.VMEM(shape, BF16)

    def reduce_buffers():
        return [
            v(2, K - 1, Z, K, R, U), v(2, Z, K, R, U), v(2, K - 1, Z, R, U), v(2, Z, R, U),
            v(2, K - 1, R, U), v(2, R, U),
        ]

    def pair_buffers():
        return [
            v(2, K - 1, 1, K, R, HD), v(2, 1, K, R, HD), v(2, K - 1, 1, R, HD), v(2, 1, R, HD),
            v(2, K - 1, 1, R, HD),
        ]

    def panel():
        return v(C, K, K, R, U)

    def pair_panel():
        return v(2, K, K, R, HD)

    scratch = (
        [v(*w_query.shape), v(*w_keyval.shape), v(*w_output.shape)]
        + [v(N, part_rows, feat), v(N, part_rows, feat)]
        + [panel(), panel(), pair_panel(), pair_panel()]
        + reduce_buffers() + reduce_buffers() + pair_buffers() + pair_buffers()
        + [pair_panel(), pair_panel(), panel(), panel()]
        + [v(N, part_rows, feat), v(N - 1, part_rows, feat)] * 2
        + [v(part_rows, feat), v(part_rows, feat)]
        + [v(*w_query.shape), v(*w_keyval.shape), v(*w_output.shape)]
        + [pltpu.SemaphoreType.DMA((SEMS,)), pltpu.SemaphoreType.DMA((SEMS,))]
        + [pltpu.SemaphoreType.DMA((10,))]
    )
    anywhere = pl.BlockSpec(memory_space=pl.ANY)
    shape = lambda a: jax.ShapeDtypeStruct(a.shape, BF16)
    return pl.pallas_call(
        functools.partial(kernel, K, N),
        out_shape=(shape(grad_out), shape(tokens), shape(w_query), shape(w_keyval), shape(w_output)),
        in_specs=[anywhere] * 5,
        out_specs=(anywhere,) * 5,
        scratch_shapes=scratch,
        compiler_params=pltpu.CompilerParams(
            collective_id=0, has_side_effects=True, vmem_limit_bytes=56 * 1024 * 1024
        ),
        name="layer",
    )(tokens, w_query, w_keyval, w_output, grad_out)


def solution(mesh):
    N, wide = mesh.shape["narrow"], mesh.shape["wide"]
    K = next(k for k in range(1, wide + 1) if k ** 3 >= wide)
    assert K ** 3 == wide
    return jax.shard_map(
        functools.partial(shards, K, N),
        mesh=mesh,
        in_specs=(
            P("narrow", "wide"),
            P("wide", "narrow"),
            P("wide", "narrow"),
            P("narrow", "wide"),
            P("narrow", "wide"),
        ),
        out_specs=(
            P("narrow", "wide"),
            P("narrow", "wide"),
            P("wide", "narrow"),
            P("wide", "narrow"),
            P("narrow", "wide"),
        ),
        check_vma=False,
    )
```

time: 1440 us -> 114 us (0.08)
  waiting for transfers between devices: 1220 us -> 0 us
  blocking collectives: 178 us -> 0 us
  Pallas kernels: 0 us -> 107 us
  matrix products: 17.6 us -> 0 us
    reduce_scatter x4 -> x0, waiting for transfers between devices: 715 us -> none  [the longest x1 352 us: shards(): lax.psum_scatter(kv_grad, 'wide', scatter_dimension=0, tiled=True)]
    unnamed x8 -> x0, waiting for transfers between devices: 299 us -> none
    all_gather x2 -> x0, waiting for transfers between devices: 203 us -> none  [the longest x1 125 us: shards(): att_panel = lax.all_gather(attended, 'wide', axis=0, tiled=True)]
    all_gather x3 -> x0, blocking collectives: 178 us -> none  [the longest x1 163 us: shards(): kv_panel = lax.all_gather(kv_own, 'wide', axis=0, tiled=True)]
    pallas_call x0 -> x1, Pallas kernels: none -> 107 us  [shards(): pl.pallas_call(functools.partial(kernel, K, N), out_shape=(shape(grad_out...]
    dot_general x12 -> x0, matrix products: 17.6 us -> none  [the longest x2 6 us: contract_cols(): lax.dot_general(left, right, (((1,), (1,)), ((), ())), preferred_element_...]
  transfers between devices with their start and end apart: 7 -> 0, of which waited for: 7 -> 0; matrix products, arithmetic and copies ran while one was open for 2% -> 0% of each run, Pallas kernels for 0% -> 0%
where the time goes in v1:
time: 114 us; the launch traced here: 113 us
  Pallas kernels  107 us (94%)
  local copies, waits for them, and re-layouts  6.17 us (5%)
    pallas_call x1, Pallas kernels, shards(): pl.pallas_call(functools.partial(kernel, K, N), out_shape=(shape(grad_out...  107 us
    unnamed x11, local copies, waits for them, and re-layouts  6.17 us

profile of v1, /device:TPU:1, one launch (start us, length us, event | category | flops | bytes accessed | tf_op | source)
XLA Modules:
  0.0 113.4 jit_solution(16160504979687267677)
XLA Ops:
  0.6 106.6 %layer.1 = (bf16[128,256]{1,0:T(8,128)(2,1)}, bf16[128,256]{1,0:T(8,128)(2,1)}, bf16[256,2048]{1,0:T(8,128)(2,1)}, bf16[256,256]{1,0:T(8,128)(2,1)}, bf16[2048,256]{1,0:T(8,128)(2,1)}) custom-call(bf16[128,256]{1,0:T(8,128)(2,1)} %tok.1, bf16[256,2048]{1,0:T(8,128)(2,1)} %wq_h.1, bf16[256,256]{1,0:T(8,128)(2,1)} %wkv_h.1, bf16[2048,256]{1,0:T(8,128)(2,1)} %wo_h.1, ...), custom_call_target="tpu_custom_call" | custom-call | tf_op jit(solution)/shard_map/layer/pallas_call | solution.py:413
  107.3 0.0 copy-start.2
  107.3 1.5 %copy.15 = bf16[128,256]{1,0:T(8,128)(2,1)} copy(bf16[128,256]{1,0:T(8,128)(2,1)} %get-tuple-element.10) | data formatting | bytes 131072
  108.8 0.0 copy-done.2
  108.8 0.6 copy.16
  109.4 0.0 copy-start.1
  109.4 0.0 copy-start
  109.4 2.4 %copy.17 = bf16[256,2048]{1,0:T(8,128)(2,1)} copy(bf16[256,2048]{1,0:T(8,128)(2,1)} %get-tuple-element.12) | data formatting | bytes 2097152
  111.8 0.0 copy-done.1
  111.8 0.7 copy.18
  112.5 0.0 copy-done
  112.5 1.0 copy.19
Async XLA Ops:
  107.3 1.5 %copy-start.2 = (bf16[128,256]{1,0:T(8,128)(2,1)S(1)}, bf16[128,256]{1,0:T(8,128)(2,1)}, u32[]{:S(2)}) copy-start(bf16[128,256]{1,0:T(8,128)(2,1)} %get-tuple-element.11) | copy-start | bytes 196612
  109.4 2.4 %copy-start.1 = (bf16[256,256]{1,0:T(8,128)(2,1)S(1)}, bf16[256,256]{1,0:T(8,128)(2,1)}, u32[]{:S(2)}) copy-start(bf16[256,256]{1,0:T(8,128)(2,1)} %get-tuple-element.13) | copy-start | bytes 393220
  109.4 3.1 %copy-start = (bf16[2048,256]{1,0:T(8,128)(2,1)S(1)}, bf16[2048,256]{1,0:T(8,128)(2,1)}, u32[]{:S(2)}) copy-start(bf16[2048,256]{1,0:T(8,128)(2,1)} %get-tuple-element.14) | copy-start | bytes 3145732

commit v2 on v0

v2 whole, which is shorter than its diff:
```python
import functools

import jax
import jax.numpy as jnp
from jax import lax
from jax.experimental import pallas as pl
from jax.experimental.pallas import tpu as pltpu
from jax.sharding import PartitionSpec as P

HD = 128
F32 = jnp.float32
BF16 = jnp.bfloat16
MESH = pl.DeviceIdType.MESH
RECV_SEMS = 130
SEND_SEMS = 24
LOCAL_SEMS = 26
PIECES = 4
REDUCE_GROUPS = ((0, 1), (1, 2), (2, 3), (3, 4))
GATHER_GROUPS = ((0, 1), (1, 2), (2, 3), (3, 4))


def mm(left, right, dims):
    return lax.dot_general(left, right, (dims, ((), ())), preferred_element_type=F32)


NN = ((1,), (0,))
NT = ((1,), (1,))
TN = ((0,), (0,))


def kernel(
    K, N, tok, wq_h, wkv_h, wo_h, gout,
    out_h, gtok_h, gwq_h, gwkv_h, gwo_h,
    wq, wkv, wo, tpan, gpan, pq, pg, pkv, pkg,
    q_far, q_mid, q_near, qs1, q2, qs2, q3, qf,
    g_far, g_mid, g_near, gs1, g2, gs2, g3, gf,
    k1, ks1, k2, ks2, k3,
    m1, ms1, m2, ms2, m3,
    kvp, kgp, kg, ap, dp, acc, o_part, o_recv, t_part, t_recv, o_out, t_out,
    tokens_t, gwq_o, gwkv_o, gwo_o,
    send_sems, recv_sems, local_sems,
):
    Z = K
    B = K // 2
    R, U = pq.shape[4], pq.shape[5]
    rows = K * K * R
    C = 2 * Z
    me = lax.axis_index("wide")
    nar = lax.axis_index("narrow")
    z, x, y = me // (K * K), (me // K) % K, me % K
    part_rows = rows // N
    both = (0, 1)
    first = ("x", "y")
    second = ("y", "x")
    spot = (x, y)
    low, high = slice(0, B), slice(B, K)

    def peer(axis, d):
        if axis == "core":
            i = nar + 1 - 2 * (nar % 2)
            return {"narrow": i}, i
        if axis == "n":
            i = (nar + d) % N
            return {"narrow": i}, i
        if axis == "z":
            i = (z + d) % K
            return {"wide": i * K * K + x * K + y}, i
        if axis == "x":
            i = (x + d) % K
            return {"wide": z * K * K + i * K + y}, i
        i = (y + d) % K
        return {"wide": z * K * K + x * K + i}, i

    count = [0]
    sends = []

    def receiver():
        count[0] += 1
        return count[0] - 1

    def remote(axis, d, src, dst, send_sem, recv_sem):
        return pltpu.make_async_remote_copy(
            src_ref=src, dst_ref=dst, send_sem=send_sems.at[send_sem],
            recv_sem=recv_sems.at[recv_sem], device_id=peer(axis, d)[0], device_id_type=MESH,
        )

    def wait_sent(n):
        i, ref = sends[n]
        remote("core", 1, ref, ref, i, 0).wait_send()

    def batch(items, gone):
        n = len(sends)
        if n >= SEND_SEMS:
            wait_sent(n - SEND_SEMS)
        i = n % SEND_SEMS
        sends.append((i, gone))
        for axis, d, src, dst, r in items:
            remote(axis, d, src, dst, i, r).start()

    def got(r, ref):
        remote("core", 1, ref, ref, 0, r).wait_recv()

    def fan(axis, src, dst, whole):
        r = receiver()
        ds = range(1, N if axis == "n" else K)
        batch([(axis, d, src(peer(axis, d)[1]), dst(d), r) for d in ds], whole)
        return r, whole

    locals_used = [0]

    def local(pairs):
        sem = local_sems.at[locals_used[0]]
        locals_used[0] += 1
        for s, d in pairs:
            pltpu.make_async_copy(s, d, sem).start()
        return sem

    def local_done(sem, ref):
        pltpu.make_async_copy(ref, ref, sem).wait()

    tok_l = local([(tok, tpan.at[nar])])
    gout_l = local([(gout, gpan.at[nar])])
    wkv_l = local([(wkv_h, wkv)])
    wq_l = local([(wq_h.at[:, c * U:(c + 1) * U], wq.at[c]) for c in range(C)])
    wo_l = local([(wo_h, wo)])

    barrier = pltpu.get_barrier_semaphore()
    peers = [("n", d) for d in range(1, N)] + [(a, d) for a in "zxy" for d in range(1, K)]
    for a, d in peers:
        pl.semaphore_signal(barrier, inc=1, device_id=peer(a, d)[0], device_id_type=MESH)
    pl.semaphore_wait(barrier, len(peers))

    def share_start(own, pan):
        far, near = receiver(), receiver()
        batch(
            [("n", 2, own, pan.at[nar], far), ("core", 1, own, pan.at[nar], near)], pan.at[0:2]
        )
        return far, near

    def share_end(pan, far, near):
        other = (nar + 2) % N
        got(far, pan.at[0])
        batch([("core", 1, pan.at[other], pan.at[other], near)], pan.at[0])
        got(near, pan.at[0:2])

    tok_c = share_start(tok, tpan)
    gout_c = share_start(gout, gpan)

    def small1(p, recv):
        out = []
        for h in both:
            src = (lambda i: p.at[h, i]) if h == 0 else (lambda i: p.at[h, :, i])
            out.append(fan(first[h], src, lambda d: recv.at[h, d - 1], recv.at[h]))
        return out

    def small2(waits, p, recv, s, recv2):
        out = []
        for h in both:
            got(*waits[h])
            total = (p[h, x] if h == 0 else p[h, :, y]).astype(F32)
            for d in range(K - 1):
                total += recv[h, d].astype(F32)
            s[h] = total.astype(BF16)
            out.append(fan(second[h], lambda i: s.at[h, i], lambda d: recv2.at[h, d - 1], recv2.at[h]))
        return out

    def small3(waits, s, recv2, t, recv3):
        out = []
        for h in both:
            got(*waits[h])
            total = s[h, spot[1 - h]].astype(F32)
            for d in range(K - 1):
                total += recv2[h, d].astype(F32)
            t[h] = total.astype(BF16)
            out.append(fan("z", lambda i: t.at[h], lambda d: recv3.at[h, d - 1], recv3.at[h]))
        return out

    def small4(waits, t, recv3, p):
        out = []
        for h in both:
            got(*waits[h])
            total = t[h].astype(F32)
            for d in range(K - 1):
                total += recv3[h, d].astype(F32)
            p[h, x, y] = total.astype(BF16)
            here = p.at[h, x, y]
            out.append(fan(second[h], lambda i: here, lambda d: here, p.at[h, 0, 1:K]))
        return out

    def small5(waits, p):
        out = []
        for h in both:
            got(*waits[h])
            here = p.at[h, x] if h == 0 else p.at[h, :, y]
            out.append(fan(first[h], lambda i: here, lambda d: here, p.at[h, 1:K]))
        return out

    def view(h, slots, i, part):
        return (h, slots, i, part) if h == 0 else (h, slots, part, i)

    class Reduce:
        groups = REDUCE_GROUPS

        def __init__(self, p, far, mid, near, s1, r2, s2, r3, f):
            self.p, self.far, self.mid, self.near = p, far, mid, near
            self.s1, self.r2, self.s2, self.r3, self.f = s1, r2, s2, r3, f
            self.c1, self.c2 = {}, {}
            self.c3 = receiver()

        def weight(self, h, e):
            return h * Z + (z + 1 + e) % K

        def start(self, n):
            slots = slice(*self.groups[n])
            for h in both:
                i = spot[h]
                there, after, before = (i + 2) % K, (i + 1) % K, (i + K - 1) % K
                axis, p = first[h], self.p
                f, r = receiver(), receiver()
                self.c1[n, h] = f, r
                batch([
                    (axis, 1, p.at[view(h, slots, there, low)], self.far.at[h, 0, slots], f),
                    (axis, K - 1, p.at[view(h, slots, there, high)], self.far.at[h, 1, slots], f),
                    (axis, 1, p.at[view(h, slots, after, high)], self.near.at[h, 0, slots, high], r),
                    (axis, K - 1, p.at[view(h, slots, before, low)], self.near.at[h, 1, slots, low], r),
                ], self.near.at[h, :, slots])

        def relay(self, n):
            slots = slice(*self.groups[n])
            for h in both:
                i = spot[h]
                f, r = self.c1[n, h]
                got(f, self.far.at[h, :, slots])
                items = []
                for side, d, part in ((0, 1, low), (1, K - 1, high)):
                    for e in range(*self.groups[n]):
                        own = self.p[view(h, e, (i + d) % K, part)].astype(F32)
                        total = own + self.far[h, side, e].astype(F32)
                        self.mid[h, side, e] = total.astype(BF16)
                    items.append((
                        first[h], d, self.mid.at[h, side, slots],
                        self.near.at[h, side, slots, part], r,
                    ))
                batch(items, self.mid.at[h, :, slots])

        def collect(self, n):
            slots = slice(*self.groups[n])
            for h in both:
                got(self.c1[n, h][1], self.near.at[h, :, slots])
                for e in range(*self.groups[n]):
                    total = self.p[view(h, e, spot[h], slice(0, K))].astype(F32)
                    total += self.near[h, 0, e].astype(F32)
                    total += self.near[h, 1, e].astype(F32)
                    self.s1[h, e] = total.astype(BF16)
                self.c2[n, h] = fan(
                    second[h], lambda i: self.s1.at[h, slots, i],
                    lambda d: self.r2.at[h, d - 1, slots], self.r2.at[h, :, slots],
                )

        def across(self, n):
            for h in both:
                got(*self.c2[n, h])
                for e in range(*self.groups[n]):
                    total = self.s1[h, e, spot[1 - h]].astype(F32)
                    for d in range(K - 1):
                        total += self.r2[h, d, e].astype(F32)
                    self.s2[h, e] = total.astype(BF16)
            items = [
                ("z", e + 1, self.s2.at[:, e], self.r3.at[e], self.c3)
                for e in range(*self.groups[n]) if e < K - 1
            ]
            if items:
                batch(items, self.r3.at[0:len(items)])

        def finish(self):
            got(self.c3, self.r3)
            total = self.s2[:, K - 1].astype(F32)
            for d in range(K - 1):
                total += self.r3[d].astype(F32)
            self.f[...] = total.astype(BF16)

    class Gather:
        groups = GATHER_GROUPS

        def __init__(self, p):
            self.p = p
            self.c1, self.c2, self.c3, self.c4 = [], {}, {}, {}

        def weight(self, h, e):
            return h * Z + (z + K - e) % K

        def start(self):
            p = self.p
            self.c1 = [receiver() for d in range(1, K)]
            batch(
                [("z", d, p.at[:, 0, x, y], p.at[:, d, x, y], self.c1[d - 1]) for d in range(1, K)],
                p.at[:, 1:K, 0, 0],
            )

        def across(self, n):
            e0, e1 = self.groups[n]
            for e in range(max(e0, 1), e1):
                got(self.c1[e - 1], self.p.at[:, e, 0, 0])
            for h in both:
                here = self.p.at[h, e0:e1, x, y]
                self.c2[n, h] = fan(
                    second[h], lambda i: here, lambda d: here, self.p.at[h, e0:e1, 0, 1:K]
                )

        def ring(self, n):
            slots = slice(*self.groups[n])
            for h in both:
                got(*self.c2[n, h])
                here = self.p.at[view(h, slots, spot[h], slice(0, K))]
                r = receiver()
                self.c3[n, h] = r
                batch([(first[h], d, here, here, r) for d in (1, K - 1)], self.p.at[h, slots, 0:2])

        def relay(self, n):
            slots = slice(*self.groups[n])
            for h in both:
                got(self.c3[n, h], self.p.at[h, slots, 0:2])
                r = receiver()
                self.c4[n, h] = r
                items = []
                for d, part in ((1, low), (K - 1, high)):
                    here = self.p.at[view(h, slots, (spot[h] + K - d) % K, part)]
                    items.append((first[h], d, here, here, r))
                batch(items, self.p.at[h, slots, 0])

        def done(self, n):
            slots = slice(*self.groups[n])
            for h in both:
                got(self.c4[n, h], self.p.at[h, slots, 0])

    def tall(pan):
        return pan[...].reshape(rows, -1)

    local_done(tok_l, tok)
    share_end(tpan, *tok_c)
    local_done(wkv_l, wkv)
    kv = mm(tall(tpan), wkv[...], NN).astype(BF16)
    for h in both:
        pkv[h] = kv[:, h * HD:(h + 1) * HD].reshape(K, K, R, HD)
    k_c = small1(pkv, k1)
    local_done(wq_l, wq)

    q = Reduce(pq, q_far, q_mid, q_near, qs1, q2, qs2, q3, qf)
    g = Reduce(pg, g_far, g_mid, g_near, gs1, g2, gs2, g3, gf)

    def project(n):
        for e in range(*q.groups[n]):
            for h in both:
                v = mm(tall(tpan), wq[q.weight(h, e)], NN)
                pq[h, e] = v.astype(BF16).reshape(K, K, R, U)

    def back_out(n):
        for e in range(*g.groups[n]):
            for h in both:
                at = pl.multiple_of(g.weight(h, e) * U, U)
                v = mm(tall(gpan), wo[pl.ds(at, U), :], NT)
                pg[h, e] = v.astype(BF16).reshape(K, K, R, U)

    G = len(REDUCE_GROUPS)
    work = [(q, n) for n in range(G)] + [(g, n) for n in range(G)]

    def step(t):
        if t < 2 * G:
            s, n = work[t]
            (project if s is q else back_out)(n)
            s.start(n)
        for lag, name in ((1, "relay"), (2, "collect"), (3, "across")):
            if 0 <= t - lag < 2 * G:
                s, n = work[t - lag]
                getattr(s, name)(n)

    def g_ready():
        share_end(gpan, *gout_c)
        local_done(gout_l, gout)
        local_done(wo_l, wo)

    def heads(f):
        return jnp.concatenate(
            [f[h, :, k * HD:(k + 1) * HD] for h in both for k in range(U // HD)], axis=0
        )

    def unheads(p, v):
        per = U // HD
        for h in both:
            p[h, 0, x, y] = jnp.concatenate(
                [v[(h * per + k) * R:(h * per + k + 1) * R] for k in range(per)], axis=1
            )

    scale = HD ** (-0.5)
    kept = {}

    def output_end():
        got(*kept["o"])
        sum_narrow(o_part, o_recv, o_out)
        store([(o_out, out_h)], o_out)

    def forward():
        q.finish()
        for h in both:
            got(*kept["k"][h])
        queries = heads(qf)
        keys = kvp[0].reshape(rows, HD)
        values = kvp[1].reshape(rows, HD)
        scores = mm(queries, keys, NT) * scale
        place = lax.broadcasted_iota(jnp.int32, scores.shape, 0) % R + (x * K + y) * R
        allowed = lax.broadcasted_iota(jnp.int32, scores.shape, 1) <= place
        weights = jnp.where(allowed, jnp.exp(scores), 0.0)
        weights = weights / jnp.sum(weights, axis=1, keepdims=True)
        probs = weights.astype(BF16)
        unheads(ap, mm(probs, values, NN).astype(BF16))
        kept["fwd"] = queries, keys, values, weights, probs

    def backward():
        g.finish()
        queries, keys, values, weights, probs = kept["fwd"]
        cotangent = heads(gf)
        prob_grad = mm(cotangent, values, NT)
        score_grad = weights * (prob_grad - jnp.sum(weights * prob_grad, axis=1, keepdims=True))
        score_half = score_grad.astype(BF16)
        unheads(dp, (mm(score_half, keys, NN) * scale).astype(BF16))
        dq.start()
        dq.across(0)
        grad_keys = mm(score_half, queries, TN) * scale
        grad_values = mm(probs, cotangent, TN)
        pkg[0] = grad_keys.astype(BF16).reshape(K, K, R, HD)
        pkg[1] = grad_values.astype(BF16).reshape(K, K, R, HD)
        kept["m"] = small1(pkg, m1)

    att = Gather(ap)
    dq = Gather(dp)
    stores = []

    def store(pairs, ref):
        stores.append((local(pairs), ref))

    def sum_narrow(part, recv, o):
        total = part[nar].astype(F32)
        for d in range(N - 1):
            total += recv[d].astype(F32)
        o[...] = total.astype(BF16)

    def w_output_grad(n):
        for e in range(*att.groups[n]):
            for h in both:
                c = att.weight(h, e)
                gwo_o[h, e] = mm(ap[h, e].reshape(rows, U), tall(gpan), TN).astype(BF16)
                store([(gwo_o.at[h, e], gwo_h.at[pl.ds(pl.multiple_of(c * U, U), U), :])], gwo_o.at[h, e])

    def w_query_grad(n):
        for e in range(*dq.groups[n]):
            for h in both:
                c = dq.weight(h, e)
                gwq_o[h, e] = mm(tokens_t[...], dp[h, e].reshape(rows, U), NN).astype(BF16)
                store([(gwq_o.at[h, e], gwq_h.at[:, pl.ds(pl.multiple_of(c * U, U), U)])], gwq_o.at[h, e])

    def add(term, start=False):
        acc[...] = term if start else acc[...] + term

    def output_part(n):
        for e in range(*att.groups[n]):
            for h in both:
                at = pl.multiple_of(att.weight(h, e) * U, U)
                add(mm(ap[h, e].reshape(rows, U), wo[pl.ds(at, U), :], NN), e == 0 and h == 0)

    def output_send():
        o_part[...] = acc[...].astype(BF16).reshape(N, part_rows, -1)
        kept["o"] = fan("n", lambda i: o_part.at[i], lambda d: o_recv.at[d - 1], o_recv)

    def kv_grad_part():
        for h in both:
            got(*kept["m"][h])
        kg[...] = jnp.concatenate([kgp[h].reshape(rows, HD) for h in both], axis=1)
        gwkv_o[...] = mm(tokens_t[...], kg[...], NN).astype(BF16)
        store([(gwkv_o, gwkv_h)], gwkv_o)
        add(mm(kg[...], wkv[...], NT), True)

    def token_grad_part(n):
        for e in range(*dq.groups[n]):
            for h in both:
                add(mm(dp[h, e].reshape(rows, U), wq[dq.weight(h, e)], NT))

    def m_2():
        kept["m"] = small2(kept["m"], pkg, m1, ms1, m2)

    def m_3():
        kept["m"] = small3(kept["m"], ms1, m2, ms2, m3)

    def m_4():
        kept["m"] = small4(kept["m"], ms2, m3, kgp)

    def m_5():
        kept["m"] = small5(kept["m"], kgp)

    def k_2():
        kept["k"] = small2(k_c, pkv, k1, ks1, k2)

    def k_3():
        kept["k"] = small3(kept["k"], ks1, k2, ks2, k3)

    def k_4():
        kept["k"] = small4(kept["k"], ks2, k3, kvp)

    def k_5():
        kept["k"] = small5(kept["k"], kvp)

    step(0)
    step(1)
    k_2()
    step(2)
    k_3()
    step(3)
    k_4()
    g_ready()
    step(4)
    k_5()
    step(5)
    step(6)
    step(7)
    forward()
    att.start()
    att.across(0)
    step(8)
    att.across(1)
    step(9)
    att.ring(0)
    att.across(2)
    step(10)
    att.across(3)
    att.ring(1)
    backward()
    att.relay(0)
    att.ring(2)
    m_2()
    dq.across(1)
    att.relay(1)
    att.ring(3)
    dq.across(2)
    m_3()
    dq.across(3)
    dq.ring(0)
    att.relay(2)
    m_4()
    dq.ring(1)
    att.relay(3)
    dq.relay(0)
    m_5()
    dq.ring(2)
    dq.relay(1)
    tokens_t[...] = tall(tpan).T
    for n in range(4):
        att.done(n)
        output_part(n)
    output_send()
    dq.ring(3)
    dq.relay(2)
    w_output_grad(0)
    w_output_grad(1)
    kv_grad_part()
    dq.relay(3)
    w_output_grad(2)
    w_output_grad(3)
    output_end()
    for n in range(4):
        dq.done(n)
        token_grad_part(n)
        if n < 3:
            w_query_grad(n)
    t_part[...] = acc[...].astype(BF16).reshape(N, part_rows, -1)
    kept["t"] = fan("n", lambda i: t_part.at[i], lambda d: t_recv.at[d - 1], t_recv)
    w_query_grad(3)

    got(*kept["t"])
    sum_narrow(t_part, t_recv, t_out)
    store([(t_out, gtok_h)], t_out)
    for sem, ref in stores:
        local_done(sem, ref)
    for n in range(max(0, len(sends) - SEND_SEMS), len(sends)):
        wait_sent(n)


def last_kernel(*refs):
    loads = []
    for src, held, dst in zip(refs[:5], refs[10:15], refs[5:10]):
        n = PIECES if src.shape[0] * src.shape[1] > 2 ** 18 else 1
        size = src.shape[0] // n
        for i in range(n):
            at = slice(i * size, (i + 1) * size)
            c = pltpu.make_async_copy(src.at[at], held.at[at], refs[15].at[len(loads)])
            c.start()
            loads.append((c, held.at[at], dst.at[at]))
    stores = []
    for c, src, dst in loads:
        c.wait()
        stores.append(pltpu.make_async_copy(src, dst, refs[16].at[len(stores)]))
        stores[-1].start()
    for c in stores:
        c.wait()


def shards(K, N, tokens, w_query, w_keyval, w_output, grad_out):
    part_rows, feat = tokens.shape
    rows = part_rows * N
    R = rows // (K * K)
    qc = w_query.shape[1]
    Z = K
    C = 2 * Z
    U = qc // C
    B = K // 2
    assert w_keyval.shape[1] == 2 * HD and U % HD == 0 and N == 4 and K == 4

    def v(*shape):
        return pltpu.VMEM(shape, BF16)

    def reduce_buffers():
        return [
            v(2, 2, K, B, R, U), v(2, 2, K, B, R, U), v(2, 2, K, K, R, U), v(2, K, K, R, U),
            v(2, K - 1, K, R, U), v(2, K, R, U), v(K - 1, 2, R, U), v(2, R, U),
        ]

    def pair_buffers():
        return [
            v(2, K - 1, K, R, HD), v(2, K, R, HD), v(2, K - 1, R, HD), v(2, R, HD),
            v(2, K - 1, R, HD),
        ]

    def panel():
        return v(2, K, K, K, R, U)

    def pair_panel():
        return v(2, K, K, R, HD)

    scratch = (
        [v(C, feat, U), v(*w_keyval.shape), v(*w_output.shape)]
        + [v(N, part_rows, feat), v(N, part_rows, feat)]
        + [panel(), panel(), pair_panel(), pair_panel()]
        + reduce_buffers() + reduce_buffers() + pair_buffers() + pair_buffers()
        + [pair_panel(), pair_panel(), v(rows, 2 * HD), panel(), panel()]
        + [pltpu.VMEM((rows, feat), F32)]
        + [v(N, part_rows, feat), v(N - 1, part_rows, feat)] * 2
        + [v(part_rows, feat), v(part_rows, feat)]
        + [v(feat, rows), v(2, K, feat, U), v(*w_keyval.shape), v(2, K, U, feat)]
        + [pltpu.SemaphoreType.DMA((SEND_SEMS,)), pltpu.SemaphoreType.DMA((RECV_SEMS,))]
        + [pltpu.SemaphoreType.DMA((LOCAL_SEMS,))]
    )
    anywhere = pl.BlockSpec(memory_space=pl.ANY)

    def array(*shape):
        return jax.ShapeDtypeStruct(shape, BF16)

    shapes = (
        array(part_rows, feat), array(part_rows, feat),
        array(feat, qc), array(feat, 2 * HD), array(qc, feat),
    )
    results = pl.pallas_call(
        functools.partial(kernel, K, N),
        out_shape=shapes,
        in_specs=[anywhere] * 5,
        out_specs=(anywhere,) * 5,
        scratch_shapes=scratch,
        compiler_params=pltpu.CompilerParams(
            collective_id=0, has_side_effects=True, vmem_limit_bytes=56 * 1024 * 1024
        ),
        name="layer",
    )(tokens, w_query, w_keyval, w_output, grad_out)
    return pl.pallas_call(
        last_kernel,
        out_shape=shapes,
        in_specs=[anywhere] * 5,
        out_specs=(anywhere,) * 5,
        scratch_shapes=[v(*s.shape) for s in shapes]
        + [pltpu.SemaphoreType.DMA((3 + 2 * PIECES,))] * 2,
        compiler_params=pltpu.CompilerParams(vmem_limit_bytes=60 * 1024 * 1024),
        name="hand_over",
    )(*results)


def solution(mesh):
    N, wide = mesh.shape["narrow"], mesh.shape["wide"]
    K = next(k for k in range(1, wide + 1) if k ** 3 >= wide)
    assert K ** 3 == wide
    return jax.shard_map(
        functools.partial(shards, K, N),
        mesh=mesh,
        in_specs=(
            P("narrow", "wide"),
            P("wide", "narrow"),
            P("wide", "narrow"),
            P("narrow", "wide"),
            P("narrow", "wide"),
        ),
        out_specs=(
            P("narrow", "wide"),
            P("narrow", "wide"),
            P("wide", "narrow"),
            P("wide", "narrow"),
            P("narrow", "wide"),
        ),
        check_vma=False,
    )
```

time: 1440 us -> 92.3 us (0.06)
  waiting for transfers between devices: 1220 us -> 0 us
  blocking collectives: 178 us -> 0 us
  Pallas kernels: 0 us -> 91.5 us
  matrix products: 17.6 us -> 0 us
    reduce_scatter x4 -> x0, waiting for transfers between devices: 715 us -> none  [the longest x1 352 us: shards(): lax.psum_scatter(kv_grad, 'wide', scatter_dimension=0, tiled=True)]
    unnamed x8 -> x0, waiting for transfers between devices: 299 us -> none
    all_gather x2 -> x0, waiting for transfers between devices: 203 us -> none  [the longest x1 125 us: shards(): att_panel = lax.all_gather(attended, 'wide', axis=0, tiled=True)]
    all_gather x3 -> x0, blocking collectives: 178 us -> none  [the longest x1 163 us: shards(): kv_panel = lax.all_gather(kv_own, 'wide', axis=0, tiled=True)]
    pallas_call x0 -> x2, Pallas kernels: none -> 91.5 us  [the longest x1 88.9 us: shards(): pl.pallas_call(functools.partial(kernel, K, N), out_shape=shapes, in_spec...]
    dot_general x12 -> x0, matrix products: 17.6 us -> none  [the longest x2 6 us: contract_cols(): lax.dot_general(left, right, (((1,), (1,)), ((), ())), preferred_element_...]
  transfers between devices with their start and end apart: 7 -> 0, of which waited for: 7 -> 0; matrix products, arithmetic and copies ran while one was open for 2% -> 0% of each run, Pallas kernels for 0% -> 0%
where the time goes in v2:
time: 92.3 us; the launch traced here: 92.2 us
  Pallas kernels  91.5 us (99%)
    pallas_call x1, Pallas kernels, shards(): pl.pallas_call(functools.partial(kernel, K, N), out_shape=shapes, in_spec...  88.9 us
    pallas_call x1, Pallas kernels, shards(): pl.pallas_call(last_kernel, out_shape=shapes, in_specs=[anywhere] * 5, ou...  2.57 us

profile of v2, /device:TPU:1, one launch (start us, length us, event | category | flops | bytes accessed | tf_op | source)
XLA Modules:
  0.0 92.2 jit_solution(5733603961198535553)
XLA Ops:
  0.6 88.9 %layer.1 = (bf16[128,256]{1,0:T(8,128)(2,1)}, bf16[128,256]{1,0:T(8,128)(2,1)}, bf16[256,2048]{1,0:T(8,128)(2,1)}, bf16[256,256]{1,0:T(8,128)(2,1)}, bf16[2048,256]{1,0:T(8,128)(2,1)}) custom-call(bf16[128,256]{1,0:T(8,128)(2,1)} %tok.1, bf16[256,2048]{1,0:T(8,128)(2,1)} %wq_h.1, bf16[256,256]{1,0:T(8,128)(2,1)} %wkv_h.1, bf16[2048,256]{1,0:T(8,128)(2,1)} %wo_h.1, ...), custom_call_target="tpu_custom_call" | custom-call | tf_op jit(solution)/shard_map/layer/pallas_call | solution.py:659
  89.6 2.6 %hand_over.1 = (bf16[128,256]{1,0:T(8,128)(2,1)}, bf16[128,256]{1,0:T(8,128)(2,1)}, bf16[256,2048]{1,0:T(8,128)(2,1)}, bf16[256,256]{1,0:T(8,128)(2,1)}, bf16[2048,256]{1,0:T(8,128)(2,1)}) custom-call(bf16[128,256]{1,0:T(8,128)(2,1)} %get-tuple-element.10.refs_0_, bf16[128,256]{1,0:T(8,128)(2,1)} %get-tuple-element.11.refs_1_, ...), custom_call_target="tpu_custom_call" | custom-call | tf_op jit(solution)/shard_map/hand_over/pallas_call | solution.py:670

commit v3 on v2

--- a/solution.py
+++ b/solution.py
@@ -12,7 +12,7 @@
 BF16 = jnp.bfloat16
 MESH = pl.DeviceIdType.MESH
 RECV_SEMS = 130
-SEND_SEMS = 24
+SEND_SEMS = 48
 LOCAL_SEMS = 26
 PIECES = 4
 REDUCE_GROUPS = ((0, 1), (1, 2), (2, 3), (3, 4))
@@ -146,18 +146,34 @@
     tok_c = share_start(tok, tpan)
     gout_c = share_start(gout, gpan)
 
+    def put(p, h, e, v):
+        v = v.astype(BF16).reshape(K, K, R, -1)
+        at = (h,) if e is None else (h, e)
+        if h == 0:
+            p[at] = v
+        else:
+            for i in range(K):
+                p[at + (slice(0, K), i)] = v[i]
+
+    def get(p, h, e):
+        at = (h,) if e is None else (h, e)
+        if h == 0:
+            return p[at].reshape(rows, -1)
+        return jnp.concatenate(
+            [p[at + (slice(0, K), i)].reshape(K * R, -1) for i in range(K)], axis=0
+        )
+
     def small1(p, recv):
         out = []
         for h in both:
-            src = (lambda i: p.at[h, i]) if h == 0 else (lambda i: p.at[h, :, i])
-            out.append(fan(first[h], src, lambda d: recv.at[h, d - 1], recv.at[h]))
+            out.append(fan(first[h], lambda i: p.at[h, i], lambda d: recv.at[h, d - 1], recv.at[h]))
         return out
 
     def small2(waits, p, recv, s, recv2):
         out = []
         for h in both:
             got(*waits[h])
-            total = (p[h, x] if h == 0 else p[h, :, y]).astype(F32)
+            total = p[h, spot[h]].astype(F32)
             for d in range(K - 1):
                 total += recv[h, d].astype(F32)
             s[h] = total.astype(BF16)
@@ -182,8 +198,8 @@
             total = t[h].astype(F32)
             for d in range(K - 1):
                 total += recv3[h, d].astype(F32)
-            p[h, x, y] = total.astype(BF16)
-            here = p.at[h, x, y]
+            p[h, spot[h], spot[1 - h]] = total.astype(BF16)
+            here = p.at[h, spot[h], spot[1 - h]]
             out.append(fan(second[h], lambda i: here, lambda d: here, p.at[h, 0, 1:K]))
         return out
 
@@ -191,12 +207,12 @@
         out = []
         for h in both:
             got(*waits[h])
-            here = p.at[h, x] if h == 0 else p.at[h, :, y]
+            here = p.at[h, spot[h]]
             out.append(fan(first[h], lambda i: here, lambda d: here, p.at[h, 1:K]))
         return out
 
     def view(h, slots, i, part):
-        return (h, slots, i, part) if h == 0 else (h, slots, part, i)
+        return (h, slots, i, part)
 
     class Reduce:
         groups = REDUCE_GROUPS
@@ -293,7 +309,11 @@
             p = self.p
             self.c1 = [receiver() for d in range(1, K)]
             batch(
-                [("z", d, p.at[:, 0, x, y], p.at[:, d, x, y], self.c1[d - 1]) for d in range(1, K)],
+                [
+                    ("z", d, p.at[h, 0, spot[h], spot[1 - h]], p.at[h, d, spot[h], spot[1 - h]],
+                     self.c1[d - 1])
+                    for d in range(1, K) for h in both
+                ],
                 p.at[:, 1:K, 0, 0],
             )
 
@@ -302,7 +322,7 @@
             for e in range(max(e0, 1), e1):
                 got(self.c1[e - 1], self.p.at[:, e, 0, 0])
             for h in both:
-                here = self.p.at[h, e0:e1, x, y]
+                here = self.p.at[h, e0:e1, spot[h], spot[1 - h]]
                 self.c2[n, h] = fan(
                     second[h], lambda i: here, lambda d: here, self.p.at[h, e0:e1, 0, 1:K]
                 )
@@ -341,7 +361,7 @@
     local_done(wkv_l, wkv)
     kv = mm(tall(tpan), wkv[...], NN).astype(BF16)
     for h in both:
-        pkv[h] = kv[:, h * HD:(h + 1) * HD].reshape(K, K, R, HD)
+        put(pkv, h, None, kv[:, h * HD:(h + 1) * HD])
     k_c = small1(pkv, k1)
     local_done(wq_l, wq)
 
@@ -351,28 +371,32 @@
     def project(n):
         for e in range(*q.groups[n]):
             for h in both:
-                v = mm(tall(tpan), wq[q.weight(h, e)], NN)
-                pq[h, e] = v.astype(BF16).reshape(K, K, R, U)
+                put(pq, h, e, mm(tall(tpan), wq[q.weight(h, e)], NN))
 
     def back_out(n):
         for e in range(*g.groups[n]):
             for h in both:
                 at = pl.multiple_of(g.weight(h, e) * U, U)
-                v = mm(tall(gpan), wo[pl.ds(at, U), :], NT)
-                pg[h, e] = v.astype(BF16).reshape(K, K, R, U)
+                put(pg, h, e, mm(tall(gpan), wo[pl.ds(at, U), :], NT))
 
     G = len(REDUCE_GROUPS)
     work = [(q, n) for n in range(G)] + [(g, n) for n in range(G)]
 
-    def step(t):
-        if t < 2 * G:
-            s, n = work[t]
-            (project if s is q else back_out)(n)
-            s.start(n)
-        for lag, name in ((1, "relay"), (2, "collect"), (3, "across")):
-            if 0 <= t - lag < 2 * G:
-                s, n = work[t - lag]
-                getattr(s, name)(n)
+    def compute(t):
+        s, n = work[t]
+        (project if s is q else back_out)(n)
+
+    def start(t):
+        work[t][0].start(work[t][1])
+
+    def relay(t):
+        work[t][0].relay(work[t][1])
+
+    def collect(t):
+        work[t][0].collect(work[t][1])
+
+    def across(t):
+        work[t][0].across(work[t][1])
 
     def g_ready():
         share_end(gpan, *gout_c)
@@ -387,7 +411,7 @@
     def unheads(p, v):
         per = U // HD
         for h in both:
-            p[h, 0, x, y] = jnp.concatenate(
+            p[h, 0, spot[h], spot[1 - h]] = jnp.concatenate(
                 [v[(h * per + k) * R:(h * per + k + 1) * R] for k in range(per)], axis=1
             )
 
@@ -404,8 +428,8 @@
         for h in both:
             got(*kept["k"][h])
         queries = heads(qf)
-        keys = kvp[0].reshape(rows, HD)
-        values = kvp[1].reshape(rows, HD)
+        keys = get(kvp, 0, None)
+        values = get(kvp, 1, None)
         scores = mm(queries, keys, NT) * scale
         place = lax.broadcasted_iota(jnp.int32, scores.shape, 0) % R + (x * K + y) * R
         allowed = lax.broadcasted_iota(jnp.int32, scores.shape, 1) <= place
@@ -427,8 +451,8 @@
         dq.across(0)
         grad_keys = mm(score_half, queries, TN) * scale
         grad_values = mm(probs, cotangent, TN)
-        pkg[0] = grad_keys.astype(BF16).reshape(K, K, R, HD)
-        pkg[1] = grad_values.astype(BF16).reshape(K, K, R, HD)
+        put(pkg, 0, None, grad_keys)
+        put(pkg, 1, None, grad_values)
         kept["m"] = small1(pkg, m1)
 
     att = Gather(ap)
@@ -448,14 +472,14 @@
         for e in range(*att.groups[n]):
             for h in both:
                 c = att.weight(h, e)
-                gwo_o[h, e] = mm(ap[h, e].reshape(rows, U), tall(gpan), TN).astype(BF16)
+                gwo_o[h, e] = mm(get(ap, h, e), tall(gpan), TN).astype(BF16)
                 store([(gwo_o.at[h, e], gwo_h.at[pl.ds(pl.multiple_of(c * U, U), U), :])], gwo_o.at[h, e])
 
     def w_query_grad(n):
         for e in range(*dq.groups[n]):
             for h in both:
                 c = dq.weight(h, e)
-                gwq_o[h, e] = mm(tokens_t[...], dp[h, e].reshape(rows, U), NN).astype(BF16)
+                gwq_o[h, e] = mm(tokens_t[...], get(dp, h, e), NN).astype(BF16)
                 store([(gwq_o.at[h, e], gwq_h.at[:, pl.ds(pl.multiple_of(c * U, U), U)])], gwq_o.at[h, e])
 
     def add(term, start=False):
@@ -465,7 +489,7 @@
         for e in range(*att.groups[n]):
             for h in both:
                 at = pl.multiple_of(att.weight(h, e) * U, U)
-                add(mm(ap[h, e].reshape(rows, U), wo[pl.ds(at, U), :], NN), e == 0 and h == 0)
+                add(mm(get(ap, h, e), wo[pl.ds(at, U), :], NN), e == 0 and h == 0)
 
     def output_send():
         o_part[...] = acc[...].astype(BF16).reshape(N, part_rows, -1)
@@ -474,7 +498,7 @@
     def kv_grad_part():
         for h in both:
             got(*kept["m"][h])
-        kg[...] = jnp.concatenate([kgp[h].reshape(rows, HD) for h in both], axis=1)
+        kg[...] = jnp.concatenate([get(kgp, h, None) for h in both], axis=1)
         gwkv_o[...] = mm(tokens_t[...], kg[...], NN).astype(BF16)
         store([(gwkv_o, gwkv_h)], gwkv_o)
         add(mm(kg[...], wkv[...], NT), True)
@@ -482,7 +506,7 @@
     def token_grad_part(n):
         for e in range(*dq.groups[n]):
             for h in both:
-                add(mm(dp[h, e].reshape(rows, U), wq[dq.weight(h, e)], NT))
+                add(mm(get(dp, h, e), wq[dq.weight(h, e)], NT))
 
     def m_2():
         kept["m"] = small2(kept["m"], pkg, m1, ms1, m2)
@@ -508,70 +532,110 @@
     def k_5():
         kept["k"] = small5(kept["k"], kvp)
 
-    step(0)
-    step(1)
+    compute(0)
+    start(0)
+    compute(1)
+    start(1)
+    compute(2)
+    start(2)
+    relay(0)
     k_2()
-    step(2)
+    compute(3)
+    start(3)
+    relay(1)
+    collect(0)
     k_3()
-    step(3)
+    g_ready()
+    compute(4)
+    start(4)
+    relay(2)
+    collect(1)
+    across(0)
     k_4()
-    g_ready()
-    step(4)
+    compute(5)
+    start(5)
+    relay(3)
+    collect(2)
+    across(1)
     k_5()
-    step(5)
-    step(6)
-    step(7)
+    compute(6)
+    start(6)
+    relay(4)
+    collect(3)
+    across(2)
+    compute(7)
+    start(7)
+    relay(5)
+    collect(4)
+    across(3)
+    relay(6)
+    collect(5)
+    across(4)
     forward()
     att.start()
     att.across(0)
-    step(8)
+    relay(7)
+    collect(6)
+    across(5)
     att.across(1)
-    step(9)
+    collect(7)
+    across(6)
     att.ring(0)
     att.across(2)
-    step(10)
+    across(7)
     att.across(3)
     att.ring(1)
     backward()
+    att.ring(2)
     att.relay(0)
-    att.ring(2)
+    att.ring(3)
     m_2()
+    att.relay(1)
     dq.across(1)
-    att.relay(1)
-    att.ring(3)
     dq.across(2)
+    dq.ring(0)
     m_3()
     dq.across(3)
-    dq.ring(0)
+    dq.ring(1)
     att.relay(2)
     m_4()
-    dq.ring(1)
+    dq.ring(2)
     att.relay(3)
     dq.relay(0)
+    dq.ring(3)
     m_5()
-    dq.ring(2)
     dq.relay(1)
+    att.done(0)
+    output_part(0)
+    att.done(1)
+    output_part(1)
+    dq.relay(2)
+    att.done(2)
+    output_part(2)
+    att.done(3)
+    output_part(3)
+    dq.relay(3)
+    output_send()
     tokens_t[...] = tall(tpan).T
-    for n in range(4):
-        att.done(n)
-        output_part(n)
-    output_send()
-    dq.ring(3)
-    dq.relay(2)
+    kv_grad_part()
+    dq.done(0)
+    token_grad_part(0)
+    dq.done(1)
+    token_grad_part(1)
+    dq.done(2)
+    token_grad_part(2)
+    dq.done(3)
+    token_grad_part(3)
+    t_part[...] = acc[...].astype(BF16).reshape(N, part_rows, -1)
+    kept["t"] = fan("n", lambda i: t_part.at[i], lambda d: t_recv.at[d - 1], t_recv)
     w_output_grad(0)
     w_output_grad(1)
-    kv_grad_part()
-    dq.relay(3)
     w_output_grad(2)
     w_output_grad(3)
     output_end()
-    for n in range(4):
-        dq.done(n)
-        token_grad_part(n)
-        if n < 3:
-            w_query_grad(n)
-    t_part[...] = acc[...].astype(BF16).reshape(N, part_rows, -1)
-    kept["t"] = fan("n", lambda i: t_part.at[i], lambda d: t_recv.at[d - 1], t_recv)
+    w_query_grad(0)
+    w_query_grad(1)
+    w_query_grad(2)
     w_query_grad(3)
 
     got(*kept["t"])

time: 92.3 us -> 88.7 us (0.961)
  Pallas kernels: 91.5 us -> 88 us
    pallas_call x1, Pallas kernels: 88.9 us -> 85.4 us  [shards(): pl.pallas_call(functools.partial(kernel, K, N), out_shape=shapes, in_spec...]
where the time goes in v3:
time: 88.7 us; the launch traced here: 88.6 us
  Pallas kernels  88 us (99%)
    pallas_call x1, Pallas kernels, shards(): pl.pallas_call(functools.partial(kernel, K, N), out_shape=shapes, in_spec...  85.4 us
    pallas_call x1, Pallas kernels, shards(): pl.pallas_call(last_kernel, out_shape=shapes, in_specs=[anywhere] * 5, ou...  2.57 us

profile of v3, /device:TPU:1, one launch (start us, length us, event | category | flops | bytes accessed | tf_op | source)
XLA Modules:
  0.0 88.6 jit_solution(1900852164005438834)
XLA Ops:
  0.6 85.4 %layer.1 = (bf16[128,256]{1,0:T(8,128)(2,1)}, bf16[128,256]{1,0:T(8,128)(2,1)}, bf16[256,2048]{1,0:T(8,128)(2,1)}, bf16[256,256]{1,0:T(8,128)(2,1)}, bf16[2048,256]{1,0:T(8,128)(2,1)}) custom-call(bf16[128,256]{1,0:T(8,128)(2,1)} %tok.1, bf16[256,2048]{1,0:T(8,128)(2,1)} %wq_h.1, bf16[256,256]{1,0:T(8,128)(2,1)} %wkv_h.1, bf16[2048,256]{1,0:T(8,128)(2,1)} %wo_h.1, ...), custom_call_target="tpu_custom_call" | custom-call | tf_op jit(solution)/shard_map/layer/pallas_call | solution.py:723
  86.1 2.6 %hand_over.1 = (bf16[128,256]{1,0:T(8,128)(2,1)}, bf16[128,256]{1,0:T(8,128)(2,1)}, bf16[256,2048]{1,0:T(8,128)(2,1)}, bf16[256,256]{1,0:T(8,128)(2,1)}, bf16[2048,256]{1,0:T(8,128)(2,1)}) custom-call(bf16[128,256]{1,0:T(8,128)(2,1)} %get-tuple-element.10.refs_0_, bf16[128,256]{1,0:T(8,128)(2,1)} %get-tuple-element.11.refs_1_, ...), custom_call_target="tpu_custom_call" | custom-call | tf_op jit(solution)/shard_map/hand_over/pallas_call | solution.py:734

commit v4 on v3

--- a/solution.py
+++ b/solution.py
@@ -358,11 +358,6 @@
 
     local_done(tok_l, tok)
     share_end(tpan, *tok_c)
-    local_done(wkv_l, wkv)
-    kv = mm(tall(tpan), wkv[...], NN).astype(BF16)
-    for h in both:
-        put(pkv, h, None, kv[:, h * HD:(h + 1) * HD])
-    k_c = small1(pkv, k1)
     local_done(wq_l, wq)
 
     q = Reduce(pq, q_far, q_mid, q_near, qs1, q2, qs2, q3, qf)
@@ -520,8 +515,15 @@
     def m_5():
         kept["m"] = small5(kept["m"], kgp)
 
+    def k_1():
+        local_done(wkv_l, wkv)
+        kv = mm(tall(tpan), wkv[...], NN)
+        for h in both:
+            put(pkv, h, None, kv[:, h * HD:(h + 1) * HD])
+        kept["k"] = small1(pkv, k1)
+
     def k_2():
-        kept["k"] = small2(k_c, pkv, k1, ks1, k2)
+        kept["k"] = small2(kept["k"], pkv, k1, ks1, k2)
 
     def k_3():
         kept["k"] = small3(kept["k"], ks1, k2, ks2, k3)
@@ -534,6 +536,7 @@
 
     compute(0)
     start(0)
+    k_1()
     compute(1)
     start(1)
     compute(2)
@@ -560,25 +563,25 @@
     k_5()
     compute(6)
     start(6)
+    collect(3)
     relay(4)
-    collect(3)
     across(2)
     compute(7)
     start(7)
+    across(3)
     relay(5)
     collect(4)
-    across(3)
     relay(6)
     collect(5)
     across(4)
+    relay(7)
     forward()
     att.start()
     att.across(0)
-    relay(7)
     collect(6)
     across(5)
+    collect(7)
     att.across(1)
-    collect(7)
     across(6)
     att.ring(0)
     att.across(2)

time: 88.7 us -> 88 us (level)
  no operation moved by 1% of the time
where the time goes in v4:
time: 88 us; the launch traced here: 87.8 us
  Pallas kernels  87.2 us (99%)
    pallas_call x1, Pallas kernels, shards(): pl.pallas_call(functools.partial(kernel, K, N), out_shape=shapes, in_spec...  84.6 us
    pallas_call x1, Pallas kernels, shards(): pl.pallas_call(last_kernel, out_shape=shapes, in_specs=[anywhere] * 5, ou...  2.57 us

profile of v4, /device:TPU:1, one launch (start us, length us, event | category | flops | bytes accessed | tf_op | source)
XLA Modules:
  0.0 87.8 jit_solution(4127091381120917614)
XLA Ops:
  0.6 84.6 %layer.1 = (bf16[128,256]{1,0:T(8,128)(2,1)}, bf16[128,256]{1,0:T(8,128)(2,1)}, bf16[256,2048]{1,0:T(8,128)(2,1)}, bf16[256,256]{1,0:T(8,128)(2,1)}, bf16[2048,256]{1,0:T(8,128)(2,1)}) custom-call(bf16[128,256]{1,0:T(8,128)(2,1)} %tok.1, bf16[256,2048]{1,0:T(8,128)(2,1)} %wq_h.1, bf16[256,256]{1,0:T(8,128)(2,1)} %wkv_h.1, bf16[2048,256]{1,0:T(8,128)(2,1)} %wo_h.1, ...), custom_call_target="tpu_custom_call" | custom-call | tf_op jit(solution)/shard_map/layer/pallas_call | solution.py:726
  85.3 2.6 %hand_over.1 = (bf16[128,256]{1,0:T(8,128)(2,1)}, bf16[128,256]{1,0:T(8,128)(2,1)}, bf16[256,2048]{1,0:T(8,128)(2,1)}, bf16[256,256]{1,0:T(8,128)(2,1)}, bf16[2048,256]{1,0:T(8,128)(2,1)}) custom-call(bf16[128,256]{1,0:T(8,128)(2,1)} %get-tuple-element.10.refs_0_, bf16[128,256]{1,0:T(8,128)(2,1)} %get-tuple-element.11.refs_1_, ...), custom_call_target="tpu_custom_call" | custom-call | tf_op jit(solution)/shard_map/hand_over/pallas_call | solution.py:737

commit v5 on v4

--- a/solution.py
+++ b/solution.py
@@ -12,8 +12,8 @@
 BF16 = jnp.bfloat16
 MESH = pl.DeviceIdType.MESH
 RECV_SEMS = 130
-SEND_SEMS = 48
-LOCAL_SEMS = 26
+SEND_SEMS = 32
+LOCAL_SEMS = 24
 PIECES = 4
 REDUCE_GROUPS = ((0, 1), (1, 2), (2, 3), (3, 4))
 GATHER_GROUPS = ((0, 1), (1, 2), (2, 3), (3, 4))

time: 88 us -> 87.7 us (level)
  no operation moved by 1% of the time
where the time goes in v5:
time: 87.7 us; the launch traced here: 87.6 us
  Pallas kernels  87 us (99%)
    pallas_call x1, Pallas kernels, shards(): pl.pallas_call(functools.partial(kernel, K, N), out_shape=shapes, in_spec...  84.4 us
    pallas_call x1, Pallas kernels, shards(): pl.pallas_call(last_kernel, out_shape=shapes, in_specs=[anywhere] * 5, ou...  2.57 us

profile of v5, /device:TPU:1, one launch (start us, length us, event | category | flops | bytes accessed | tf_op | source)
XLA Modules:
  0.0 87.6 jit_solution(10859776471119976157)
XLA Ops:
  0.6 84.4 %layer.1 = (bf16[128,256]{1,0:T(8,128)(2,1)}, bf16[128,256]{1,0:T(8,128)(2,1)}, bf16[256,2048]{1,0:T(8,128)(2,1)}, bf16[256,256]{1,0:T(8,128)(2,1)}, bf16[2048,256]{1,0:T(8,128)(2,1)}) custom-call(bf16[128,256]{1,0:T(8,128)(2,1)} %tok.1, bf16[256,2048]{1,0:T(8,128)(2,1)} %wq_h.1, bf16[256,256]{1,0:T(8,128)(2,1)} %wkv_h.1, bf16[2048,256]{1,0:T(8,128)(2,1)} %wo_h.1, ...), custom_call_target="tpu_custom_call" | custom-call | tf_op jit(solution)/shard_map/layer/pallas_call | solution.py:726
  85.0 2.6 %hand_over.1 = (bf16[128,256]{1,0:T(8,128)(2,1)}, bf16[128,256]{1,0:T(8,128)(2,1)}, bf16[256,2048]{1,0:T(8,128)(2,1)}, bf16[256,256]{1,0:T(8,128)(2,1)}, bf16[2048,256]{1,0:T(8,128)(2,1)}) custom-call(bf16[128,256]{1,0:T(8,128)(2,1)} %get-tuple-element.10.refs_0_, bf16[128,256]{1,0:T(8,128)(2,1)} %get-tuple-element.11.refs_1_, ...), custom_call_target="tpu_custom_call" | custom-call | tf_op jit(solution)/shard_map/hand_over/pallas_call | solution.py:737
